TPU v7x, 256 devices: a whole 4x4x8 slice. The times are simulated.
256 devices in a mesh: row: 4 (over x), col: 16 (over y_lo, z), rep: 4 (over y_hi, core).
Axes of the slice: x: 4, y: 4 (y_hi: 2, y_lo: 2; y = y_hi * 2 + y_lo), z: 8, core: 2. Of those that a mesh axis runs over, the one named last changes fastest.
Arguments:
- a_vals: float32 [96, 12, 128, 128], P('col', 'row'), may hold values from -6 to 6
- a_group: int32 [96, 12, 1], P('col', 'row'), may hold values from 0 to 63; in each aligned block of 72 rows (0 to 71, 72 to 143, ..., all dimensions but the last counted through in order) at most 2 rows name the same one
- a_offset: int32 [96, 12], P('col', 'row'), may hold values from 0 to 4
- b_vals: float32 [320, 4, 3, 128, 128], P(('col', 'rep'), 'row'), may hold values from -0.5 to 0.5
- b_cols: int32 [320, 4, 3], P(('col', 'rep'), 'row'), may hold values from 0 to 15
- c_cols: int32 [96, 4, 4], P('col', 'row'), may hold values from 0 to 15, as said below
Outputs:
- c_vals: float32 [96, 4, 4, 128, 128], P('col', 'row', 'rep')
Inputs may be any that keep to these rules, and one draw needn't show every extreme that they name: `a_group`: among the 72 stored A blocks of each aligned set of 6 block rows, at most 2 share one group, and 2 is reached. The 4 entries of c_cols[i, r] are distinct.
All inputs are finite; a program needn't handle non-finite values.
Results may differ from a plain program's by a relative error of at most 0.0003.
Values sent between devices are 32-bit elements; how exact they have to be, the bound alone decides.
A program may use at most 192 MiB of HBM per device.

v0:
```python
import jax
import jax.numpy as jnp
from jax import lax
from jax.sharding import PartitionSpec as P


def build_lists(step_of, n_steps, capacity, total):
    keys = step_of * (total + 1) + jnp.arange(total, dtype=jnp.int32)
    ordered = jnp.argsort(keys)
    tallies = jnp.sum(
        (step_of[None, :] == jnp.arange(n_steps, dtype=jnp.int32)[:, None]).astype(jnp.int32),
        axis=1,
    )
    begins = jnp.cumsum(tallies) - tallies
    places = jnp.clip(
        begins[:, None] + jnp.arange(capacity, dtype=jnp.int32)[None, :], 0, total - 1
    )
    taken = ordered[places]
    return jnp.where(
        jnp.arange(capacity, dtype=jnp.int32)[None, :] < tallies[:, None], taken, total
    )


def add_products(
    totals,
    flat_blocks,
    owner_row,
    picked,
    b_blocks,
    b_targets,
    wanted_ext,
    slot_count,
    dummy_target,
):
    products = jnp.einsum(
        "xab,xtbc->xtac", flat_blocks[picked], b_blocks, precision=lax.Precision.HIGHEST
    )
    owners = owner_row[picked]
    hitting = b_targets[:, :, None] == wanted_ext[owners][:, None, :]
    slot_index = jnp.sum(
        jnp.where(hitting, jnp.arange(slot_count, dtype=jnp.int32)[None, None, :], 0), axis=2
    )
    located = jnp.any(hitting, axis=2)
    targets = jnp.where(located, owners[:, None] * slot_count + slot_index, dummy_target)
    flat_products = products.reshape(-1, products.shape[2], products.shape[3])
    return totals.at[targets.reshape(-1)].add(flat_products)


def make_adder(
    flat_blocks,
    row_inside,
    owner_row,
    chosen,
    wanted_ext,
    row_group,
    capacity,
    slot_count,
    dummy_target,
):

    def add_piece(totals, piece, begin_row):
        piece_vals, piece_cols = piece
        span_count = piece_vals.shape[0] // row_group
        first_step = begin_row // row_group
        steps_here = jnp.arange(span_count, dtype=jnp.int32)
        picked = chosen[steps_here].reshape(-1)
        local_rows = (
            jnp.repeat(jnp.arange(span_count, dtype=jnp.int32), capacity) * row_group
            + row_inside[picked]
        )
        b_blocks = piece_vals[local_rows, 0]
        b_targets = piece_cols[local_rows, 0]
        return add_products(
            totals,
            flat_blocks,
            owner_row,
            picked,
            b_blocks,
            b_targets,
            wanted_ext,
            slot_count,
            dummy_target,
        )

    return add_piece


def local(a_vals, a_group, a_offset, b_vals, b_cols, c_cols):
    own_rep = lax.axis_index("rep")
    reps = lax.axis_size("rep")
    col_count = lax.axis_size("col")
    row_group = b_vals.shape[0]
    block_size = a_vals.shape[2]
    local_cols = a_group[:, :, 0] * row_group + a_offset
    a_all, a_cols = (
        lax.all_gather(a_vals, "row", axis=1, tiled=True),
        lax.all_gather(local_cols, "row", axis=1, tiled=True),
    )
    row_count, slots = a_cols.shape
    total = row_count * slots
    flat_blocks = jnp.concatenate(
        [
            a_all.reshape(total, block_size, block_size),
            jnp.zeros((1, block_size, block_size), jnp.float32),
        ],
        axis=0,
    )
    flat_cols = a_cols.reshape(total)
    groups_of = flat_cols // row_group
    row_inside = jnp.concatenate([flat_cols % row_group, jnp.zeros((1,), jnp.int32)])
    owner_row = jnp.concatenate(
        [jnp.arange(total, dtype=jnp.int32) // slots, jnp.full((1,), row_count, jnp.int32)]
    )
    wanted = c_cols[:, 0, :]
    slot_total = wanted.shape[1]
    share = slot_total // reps
    capacity = max(2, 2 * total // (col_count * reps))
    matches = groups_of % reps == own_rep
    step_of = jnp.where(matches, groups_of // reps, col_count).astype(jnp.int32)
    chosen = build_lists(step_of, col_count, capacity, total)
    wanted_ext = jnp.concatenate([wanted, jnp.full((1, slot_total), -1, jnp.int32)], axis=0)
    dummy_target = row_count * slot_total
    start_totals = jnp.zeros((dummy_target + 1, block_size, block_size), jnp.float32)
    adder = make_adder(
        flat_blocks,
        row_inside,
        owner_row,
        chosen,
        wanted_ext,
        row_group,
        capacity,
        slot_total,
        dummy_target,
    )
    totals = adder(
        start_totals,
        (
            lax.all_gather(b_vals, "col", axis=0, tiled=True),
            lax.all_gather(b_cols, "col", axis=0, tiled=True),
        ),
        jnp.int32(0),
    )
    partial_value = totals[:dummy_target].reshape(row_count, slot_total, block_size, block_size)
    summed = lax.psum(partial_value, "rep")
    mine = lax.dynamic_slice_in_dim(summed, own_rep * share, share, 1)
    return mine.reshape(row_count, 1, share, block_size, block_size)


def solution(mesh):
    placed = (
        P("col", "row", None, None),
        P("col", "row", None),
        P("col", "row"),
        P(("col", "rep"), "row", None, None, None),
        P(("col", "rep"), "row", None),
        P("col", "row", None),
    )
    return jax.shard_map(
        local,
        mesh=mesh,
        in_specs=placed,
        out_specs=P("col", "row", "rep", None, None),
        check_vma=False,
    )
```

profile of v0, /device:TPU:1, one launch (start us, length us, event | category | flops | bytes accessed | tf_op | source)
XLA Modules:
  0.0 351.2 jit_solution(10003853787227473209)
XLA Ops:
  6.5 0.7 all-gather.6.cloned.1.call-update
  7.3 0.7 all-gather.4.cloned.1.call-update
  8.1 0.7 broadcast_multiply_fusion
  8.8 0.7 fusion.4
  9.4 9.2 %all-gather = s32[4,3,6]{2,1,0:T(4,128)S(1)} all-gather(s32[1,3,6]{2,1,0:T(4,128)S(1)} %fusion.4), channel_id=1, replica_groups=mesh['row'=4,'col'=16,'rep'=4] {'row'}, dimensions={0}, use_global_device_ids=true | all-gather | bytes 360 | tf_op jit(solution)/shard_map/all_gather | solution.py:97
  18.9 0.1 copy.31
  19.1 0.1 copy.32
  19.3 0.1 convert_reduce_fusion
  19.6 0.1 reduce
  19.8 0.1 reshape.268
  19.9 2.5 sort.17
  22.4 0.7 gather_fusion
  23.3 0.6 gather_fusion.1
  24.1 0.1 copy.30
  24.2 0.7 gather_fusion.2
  24.9 29.7 %all_gather.12 = s32[80,1,3]{2,1,0:T(1,128)S(1)} all-gather(s32[5,1,3]{2,1,0:T(1,128)S(1)} %copy.30), channel_id=1, replica_groups=mesh['row'=4,'col'=16,'rep'=4] {'col'}, dimensions={0}, use_global_device_ids=true | all-gather | bytes 1020 | tf_op jit(solution)/shard_map/all_gather | solution.py:139
  54.6 0.6 gather_fusion.3
  55.4 0.7 gather_fusion.4
  56.2 0.6 gather_fusion.5
  57.0 0.1 select_n.135
  57.2 10.6 %all-gather.6.cloned.1.call-done = f32[6,12,128,128]{3,2,1,0:T(8,128)} async-done(((f32[6,3,128,128]{3,2,1,0:T(8,128)}), f32[6,12,128,128]{3,2,1,0:T(8,128)}) %all-gather.6.cloned.1.call-update) | async-done | bytes 4718608 | tf_op jit(solution)/shard_map/all_gather | solution.py:96
  67.7 5.1 %concatenate.20 = f32[73,128,128]{2,1,0:T(8,128)} pad(f32[72,128,128]{2,1,0:T(8,128)} %bitcast.44, f32[]{:T(128)} %constant.41.clone.1), padding=0_1x0_0x0_0 | pad | bytes 9502724 | tf_op jit(solution)/shard_map/concatenate | solution.py:101
  72.8 3.0 gather_fusion.7
  75.8 169.4 %all-gather.4.cloned.1.call-done = f32[80,1,3,128,128]{4,3,2,1,0:T(8,128)} async-done(((f32[5,1,3,128,128]{4,3,2,1,0:T(8,128)}), f32[80,1,3,128,128]{4,3,2,1,0:T(8,128)}) %all-gather.4.cloned.1.call-update) | async-done | bytes 15728656 | tf_op jit(solution)/shard_map/all_gather | solution.py:138
  245.2 9.0 %gather_fusion.6 = f32[32,3,128,128]{3,2,1,0:T(8,128)} fusion(f32[80,1,3,128,128]{4,3,2,1,0:T(8,128)} %all-gather.4.cloned.1.call-done, s32[32]{0:T(128)S(1)} %fusion.8), kind=kCustom, calls=%fused_computation.6 | custom fusion | bytes 12583168 | tf_op jit(solution)/shard_map/gather | solution.py:71
  254.2 13.4 %fusion = f32[32,3,128,128]{3,2,1,0:T(8,128)} fusion(f32[32,3,128,128]{3,2,1,0:T(8,128)} %gather_fusion.6, f32[32,128,128]{2,1,0:T(8,128)S(1)} %gather_fusion.7), kind=kOutput, calls=%fused_computation.9 | convolution fusion | flops 2415919104 | bytes 14680064 | tf_op jit(solution)/shard_map/xab,xtbc->xtac/dot_general | solution.py:35
  267.6 6.5 %copy.40 = f32[96,128,128]{2,1,0:T(8,128)} copy(f32[96,128,128]{1,2,0:T(8,128)} %bitcast.42) | data formatting | bytes 12582912 | tf_op jit(solution)/shard_map/reshape | solution.py:45
  274.2 0.2 broadcast_in_dim.21
  274.3 12.9 %scatter_fusion = f32[25,128,128]{2,1,0:T(8,128)S(1)} fusion(f32[25,128,128]{2,1,0:T(8,128)S(1)} %broadcast_in_dim.21, s32[96]{0:T(128)S(1)} %fusion.10, f32[96,128,128]{2,1,0:T(8,128)} %copy.40), kind=kCustom, calls=%fused_computation.8 | custom fusion | flops 1572864 | bytes 18874752 | tf_op jit(solution)/shard_map/scatter-add | solution.py:46
  287.2 1.3 slice.20
  288.5 54.4 %all-reduce.5.cloned.1.call-done = f32[6,4,128,128]{3,2,1,0:T(8,128)} async-done(((f32[6,4,128,128]{3,2,1,0:T(8,128)}), f32[6,4,128,128]{3,2,1,0:T(8,128)}) %all-reduce.5.cloned.1.call-update) | async-done | bytes 1572880 | tf_op jit(solution)/shard_map/psum | solution.py:144
  342.9 1.8 dynamic-slice_bitcast_fusion
  (49 shorter events, 1.7 us)
Async XLA Ops:
  6.5 61.2 %all-gather.6.cloned.1.call-start = ((), (), s32[]{:S(2)}) async-start(), calls=%async_computation.1 | async-start | bytes 5898240 | tf_op jit(solution)/shard_map/all_gather | solution.py:96
  7.3 16.8 %copy-start.1 = (s32[5,1,3]{0,1,2:T(1,128)S(1)}, s32[5,1,3]{0,1,2:T(1,128)}, u32[]{:S(2)}) copy-start(s32[5,1,3]{0,1,2:T(1,128)} %param.10) | copy-start | bytes 184
  7.3 237.9 %all-gather.4.cloned.1.call-start = ((), (), s32[]{:S(2)}) async-start(), calls=%async_computation | async-start | bytes 16711680 | tf_op jit(solution)/shard_map/all_gather | solution.py:138
  8.0 334.9 %all-reduce.5.cloned.1.call-start = ((), (), s32[]{:S(2)}) async-start(), calls=%async_computation.2 | async-start | bytes 3145728 | tf_op jit(solution)/shard_map/psum | solution.py:144
  22.4 33.7 %copy-start = (s32[6,1,4]{0,2,1:T(4,128)S(1)}, s32[6,1,4]{0,2,1:T(4,128)}, u32[]{:S(2)}) copy-start(s32[6,1,4]{0,2,1:T(4,128)} %param.11) | copy-start | bytes 292
Sparse Core Ops, SparseCore 0:
  9.2 58.5 all-gather.5
  69.5 175.6 all-gather.3
  288.6 54.2 all-reduce.4
where the time goes:
time: 352 us; the launch traced here: 351 us
  waiting for transfers between devices  236 us (67%)
  blocking collectives  38.9 us (11%)
  local copies, waits for them, and re-layouts  32.2 us (9%)
  other arithmetic  17.5 us (5%)
  matrix products  13.4 us (4%)
  between operations  13.3 us (4%)
    all_gather x1, waiting for transfers between devices, local(): lax.all_gather(b_vals, 'col', axis=0, tiled=True)  169 us
    psum x1, waiting for transfers between devices, local(): summed = lax.psum(partial_value, 'rep')  54.4 us
    all_gather x1, blocking collectives, local(): lax.all_gather(b_cols, 'col', axis=0, tiled=True)  29.7 us
    dot_general x1, matrix products, add_products(): jnp.einsum('xab,xtbc->xtac', flat_blocks[picked], b_blocks, precision=lax...  13.4 us
    scatter-add x1, other arithmetic, add_products(): return totals.at[targets.reshape(-1)].add(flat_products)  12.9 us
    all_gather x1, waiting for transfers between devices, local(): lax.all_gather(a_vals, 'row', axis=1, tiled=True)  10.6 us
    all_gather x1, blocking collectives, local(): lax.all_gather(local_cols, 'row', axis=1, tiled=True)  9.25 us
    gather x1, local copies, waits for them, and re-layouts, add_piece(): b_blocks = piece_vals[local_rows, 0]  9.05 us
  transfers between devices with their start and end apart: 3, of which 3 were waited for; matrix products, arithmetic and copies ran while one was open for 5% of the time, Pallas kernels for 0%

commit v1 on v0

v1 whole, which is shorter than its diff:
```python
import functools
import jax
import jax.numpy as jnp
from jax import lax
from jax.experimental import pallas as pl
from jax.experimental.pallas import tpu as pltpu
from jax.sharding import PartitionSpec as P

NZ = 8
NX = 4
PIECES = ((0, 4), (4, 8), (8, 12), (12, 15))
PLUS_ORDER = (0, 1, 2, 3)
MINUS_ORDER = (2, 3, 0, 1)
ROWS = 6
SLOTS = 3
KEPT = 4
TERMS = 3


def kernel(
    meta_ref, a_ref, b_ref, out_ref,
    b0, b1, b2, b3, b4, b5, b6, b7,
    a_all, acc, prod, half, far_in, near_in,
    meta_a, meta_b, table_v, table_s,
    loc_sem, tab_sem,
    ma_send, ma_recv, mb_send, mb_recv,
    bp_send, bp_recv, bm_send, bm_recv,
    y_send, y_recv, x_send, x_recv, t_send, t_recv,
    c_send, c_recv, r_send, r_recv,
):
    bufs = (b0, b1, b2, b3, b4, b5, b6, b7)
    x = lax.axis_index("row")
    col = lax.axis_index("col")
    rep = lax.axis_index("rep")
    z, y_lo = col % NZ, col // NZ
    core, y_hi = rep % 2, rep // 2
    y = y_hi * 2 + y_lo

    def at(x_, y_, z_, core_):
        return (x_, (y_ % 2) * NZ + z_, (y_ // 2) * 2 + core_)

    def z_at(step):
        return at(x, y, (z + step) % NZ, core)

    def x_at(step):
        return at((x + step) % NX, y, z, core)

    def y_at(step):
        return at(x, (y + step) % 4, z, core)

    sibling = at(x, y, z, 1 - core)
    y_pair = y_hi * 2 + (1 - y_lo)

    def copy(src, dst, send, recv, device):
        return pltpu.make_async_remote_copy(
            src_ref=src, dst_ref=dst, send_sem=send, recv_sem=recv,
            device_id=device, device_id_type=pl.DeviceIdType.MESH,
        )

    pairs = [(fy, rx) for fy in range(2) for rx in range(NX) if (fy, rx) != (0, 0)]

    def pair_at(fy, rx):
        return at((x + rx) % NX, y_hi * 2 + (y_lo + fy) % 2, z, core)

    peers = [z_at(r) for r in range(1, NZ)] + [pair_at(*p) for p in pairs]
    other_y = at(x, (y + 3 - 2 * y_lo) % 4, z, core)
    peers += [other_y, sibling]
    barrier = pltpu.get_barrier_semaphore()
    for peer in peers:
        pl.semaphore_signal(barrier, inc=1, device_id=peer, device_id_type=pl.DeviceIdType.MESH)
    pl.semaphore_wait(barrier, len(peers))

    sent = []

    def go(c):
        c.start()
        sent.append(c)
        return c

    to_z = [go(copy(meta_ref, meta_b.at[r], mb_send.at[r], mb_recv.at[r], z_at(r))) for r in range(1, NZ)]
    to_pair = [
        go(copy(meta_ref, meta_a.at[fy * NX + rx], ma_send.at[fy * NX + rx], ma_recv.at[fy * NX + rx], pair_at(fy, rx)))
        for fy, rx in pairs
    ]

    def ring(sign):
        sems = (bp_send, bp_recv) if sign > 0 else (bm_send, bm_recv)
        order = PLUS_ORDER if sign > 0 else MINUS_ORDER

        def hop(k, n):
            lo, hi = PIECES[order[n]]
            src = b_ref if k == 0 else bufs[(-sign * k) % NZ]
            dst = bufs[(-sign * (k + 1)) % NZ]
            return copy(
                src.at[pl.ds(lo, hi - lo)], dst.at[pl.ds(lo, hi - lo)],
                sems[0].at[k * 4 + n], sems[1].at[k * 4 + n], z_at(sign),
            )

        return hop

    plus, minus = ring(1), ring(-1)
    hops = {}
    for n in range(4):
        hops[1, 0, n] = go(plus(0, n))
        hops[-1, 0, n] = go(minus(0, n))

    own_b = pltpu.make_async_copy(b_ref, b0, loc_sem.at[0])
    own_b.start()
    span = ROWS * SLOTS
    cut = span // 2
    own_a = pltpu.make_async_copy(a_ref, a_all.at[pl.ds(0, span)], loc_sem.at[1])
    cross_a = copy(a_ref, a_all.at[pl.ds(0, span)], y_send, y_recv, at(x, y_pair, z, core))

    @pl.when(core == 0)
    def _():
        own_a.start()

    @pl.when(core == 1)
    def _():
        cross_a.start()

    meta_b[0] = meta_ref[...]
    meta_a[0] = meta_ref[...]
    for c in to_z + to_pair:
        c.wait_recv()
    lane = lax.broadcasted_iota(jnp.int32, (8, 128), 1)
    line = lax.broadcasted_iota(jnp.int32, (8, 128), 0)
    b_cols = jnp.concatenate([meta_b[(NZ - d) % NZ, 1:2, :] for d in range(NZ)], axis=0)
    away = (lane // 32 - x + NX) % NX
    inside = lane % 32
    place = jnp.where(away == 0, 0, jnp.where(away == 3, 1, jnp.where(away == 1, 2, 3))) * span + inside
    owner = jnp.zeros((8, 128), jnp.int32)
    for m in range(1, ROWS):
        owner = owner + jnp.where(inside >= SLOTS * m, 1, 0)
    group = (y_lo * NZ + (line + z) % NZ) * 4 + rep

    def pick(where, value):
        return jnp.sum(jnp.where(where, value, 0), axis=1, keepdims=True)

    for s in range(2):
        flip = (core + s) % 2
        base = flip * NX
        codes = meta_a[base, 0:1, :]
        for rx in range(1, NX):
            codes = codes + meta_a[base + rx, 0:1, :]
        codes = jnp.broadcast_to(codes, (8, 128)) - 1
        wanted = jnp.broadcast_to(meta_a[base, 2:3, :], (8, 128))
        match = (codes >= 0) & (codes // 8 == group)
        first = jnp.min(jnp.where(match, lane, 1000), axis=1, keepdims=True)
        last = jnp.max(jnp.where(match, lane, -1), axis=1, keepdims=True)
        result = jnp.zeros((8, 128), jnp.int32)
        for k in range(2):
            chosen = match & (lane == first) if k == 0 else match & (lane == last) & (lane != first)
            exists = pick(chosen, 1)
            index = pick(chosen, place + s * NX * span)
            offset = pick(chosen, codes % 8)
            row = pick(chosen, owner)
            result = result + jnp.where(lane == k * 32, index, 0)
            result = result + jnp.where(lane == k * 32 + 1, offset * TERMS, 0)
            result = result + jnp.where(lane == k * 32 + 2, row, 0)
            kept = [pick(lane == row * KEPT + q, wanted) for q in range(KEPT)]
            for t in range(TERMS):
                target = pick(lane == offset * TERMS + t, b_cols)
                for q in range(KEPT):
                    hit = jnp.where((target == kept[q]) & (exists > 0), 1, 0)
                    result = result + jnp.where(lane == k * 32 + 8 + t * KEPT + q, hit, 0)
        table_v[s] = result
    to_scalar = pltpu.make_async_copy(table_v, table_s, tab_sem)
    to_scalar.start()
    to_scalar.wait()

    @pl.when(core == 0)
    def _():
        own_a.wait()

    @pl.when(core == 1)
    def _():
        cross_a.wait_recv()

    def a_part(slot, lo, hi):
        return a_all.at[pl.ds(slot * span + lo, hi - lo)]

    xs = [
        copy(a_part(0, 0, cut), a_part(1, 0, cut), x_send.at[0], x_recv.at[0], x_at(1)),
        copy(a_part(0, cut, span), a_part(2, cut, span), x_send.at[1], x_recv.at[1], x_at(NX - 1)),
        copy(a_part(0, cut, span), a_part(1, cut, span), x_send.at[2], x_recv.at[2], x_at(1)),
        copy(a_part(0, 0, cut), a_part(2, 0, cut), x_send.at[3], x_recv.at[3], x_at(NX - 1)),
        copy(a_part(1, 0, cut), a_part(3, 0, cut), x_send.at[4], x_recv.at[4], x_at(1)),
        copy(a_part(2, cut, span), a_part(3, cut, span), x_send.at[5], x_recv.at[5], x_at(NX - 1)),
    ]
    ts = [
        copy(a_part(k, 0, span), a_part(NX + k, 0, span), t_send.at[k], t_recv.at[k], sibling)
        for k in range(NX)
    ]
    for c in xs[:4]:
        go(c)
    go(ts[0])

    def forward(k, n, p_on=True, m_on=True):
        hops[1, k - 1, n].wait_recv()
        if p_on:
            hops[1, k, n] = go(plus(k, n))
        hops[-1, k - 1, n].wait_recv()
        if m_on:
            hops[-1, k, n] = go(minus(k, n))

    for n in range(4):
        forward(1, n)
    xs[0].wait_recv()
    go(xs[4])
    xs[1].wait_recv()
    go(xs[5])
    xs[2].wait_recv()
    go(ts[1])
    xs[3].wait_recv()
    go(ts[2])
    for n in range(4):
        forward(2, n)
    xs[4].wait_recv()
    xs[5].wait_recv()
    go(ts[3])
    for c in ts:
        c.wait_recv()
    own_b.wait()

    def multiply(d, fresh):
        buf = bufs[d]

        def stream(s, carry):
            base = ((y_lo + core + s) % 2) * KEPT * ROWS
            for k in range(2):
                a = a_all[table_s[s, d, k * 32]]
                offset = table_s[s, d, k * 32 + 1]
                terms = [buf[offset + t] for t in range(TERMS)]
                chosen = []
                for q in range(KEPT):
                    weights = [table_s[s, d, k * 32 + 8 + t * KEPT + q].astype(jnp.float32) for t in range(TERMS)]
                    chosen.append(weights[0] * terms[0] + weights[1] * terms[1] + weights[2] * terms[2])
                b = jnp.concatenate(chosen, axis=1)
                a_hi = a.astype(jnp.bfloat16)
                a_lo = (a - a_hi.astype(jnp.float32)).astype(jnp.bfloat16)
                b_hi = b.astype(jnp.bfloat16)
                b_lo = (b - b_hi.astype(jnp.float32)).astype(jnp.bfloat16)
                dot = functools.partial(jnp.dot, preferred_element_type=jnp.float32)
                prod[k] = dot(a_hi, b_hi) + (dot(a_hi, b_lo) + dot(a_lo, b_hi))
            rows = [table_s[s, d, k * 32 + 2] for k in range(2)]

            def update(i, carry):
                w0 = jnp.where(rows[0] == i, 1.0, 0.0).astype(jnp.float32)
                w1 = jnp.where(rows[1] == i, 1.0, 0.0).astype(jnp.float32)
                for q in range(KEPT):
                    cols = pl.ds(q * 128, 128)
                    term = w0 * prod[0, :, cols] + w1 * prod[1, :, cols]
                    where = base + q * ROWS + i
                    acc[where] = term if fresh else acc[where] + term
                return carry

            return lax.fori_loop(0, ROWS, update, carry)

        lax.fori_loop(0, 2, stream, 0)

    multiply(0, True)
    forward(3, 0)
    multiply(1, False)
    forward(3, 1)
    multiply(7, False)
    forward(3, 2, False, False)
    multiply(2, False)
    multiply(6, False)
    forward(3, 3, False, False)
    multiply(3, False)
    multiply(5, False)
    for n in range(2):
        hops[1, 3, n].wait_recv()
        hops[-1, 3, n].wait_recv()
    multiply(4, False)

    def mine(step, which):
        dest = (y + step) % 4
        q = (dest // 2) * 2 + which
        return ((dest % 2) * KEPT + q) * ROWS

    cores = {}
    for step in (2, 1, 3, 0):
        cores[step] = go(copy(
            acc.at[pl.ds(mine(step, 1 - core), ROWS)], half.at[pl.ds(step * ROWS, ROWS)],
            c_send.at[step], c_recv.at[step], sibling,
        ))
    mid = ROWS // 2

    def fold(step):
        cores[step].wait_recv()
        start = mine(step, core)
        for i in range(ROWS):
            half[step * ROWS + i] = half[step * ROWS + i] + acc[start + i]

    def part(step, lo, hi):
        return half.at[pl.ds(step * ROWS + lo, hi - lo)]

    fold(2)
    far = [
        go(copy(part(2, 0, mid), far_in.at[pl.ds(0, mid)], r_send.at[0], r_recv.at[0], y_at(1))),
        go(copy(part(2, mid, ROWS), far_in.at[pl.ds(mid, ROWS - mid)], r_send.at[1], r_recv.at[1], y_at(3))),
    ]
    fold(1)
    near = [go(copy(part(1, mid, ROWS), near_in.at[pl.ds(mid, ROWS - mid)], r_send.at[2], r_recv.at[2], y_at(1)))]
    fold(3)
    near.append(go(copy(part(3, 0, mid), near_in.at[pl.ds(ROWS, mid)], r_send.at[3], r_recv.at[3], y_at(3))))
    fold(0)
    far[0].wait_recv()
    for i in range(mid):
        half[ROWS + i] = half[ROWS + i] + far_in[i]
    near.append(go(copy(part(1, 0, mid), near_in.at[pl.ds(0, mid)], r_send.at[4], r_recv.at[4], y_at(1))))
    far[1].wait_recv()
    for i in range(mid, ROWS):
        half[3 * ROWS + i] = half[3 * ROWS + i] + far_in[i]
    near.append(go(copy(part(3, mid, ROWS), near_in.at[pl.ds(ROWS + mid, ROWS - mid)], r_send.at[5], r_recv.at[5], y_at(3))))
    for c in near:
        c.wait_recv()
    for i in range(ROWS):
        out_ref[i] = half[i] + near_in[i] + near_in[ROWS + i]

    for c in sent:
        c.wait_send()

    @pl.when(core == 1)
    def _():
        cross_a.wait_send()


def local(a_vals, a_group, a_offset, b_vals, b_cols, c_cols):
    x = lax.axis_index("row")
    codes = (a_group[:, :, 0] * 8 + a_offset + 1).reshape(-1)
    lanes = jnp.arange(128, dtype=jnp.int32)
    codes = jnp.where(lanes // 32 == x, jnp.tile(jnp.pad(codes, (0, 32 - codes.shape[0])), 4), 0)
    meta = jnp.stack([
        codes,
        jnp.pad(b_cols.reshape(-1), (0, 128 - b_cols.size)),
        jnp.pad(c_cols.reshape(-1), (0, 128 - c_cols.size)),
    ])
    meta = jnp.pad(meta, ((0, 5), (0, 0)))
    a = a_vals.reshape(-1, 128, 128)
    b = b_vals.reshape(-1, 128, 128)
    blocks = lambda n: pltpu.VMEM((n, 128, 128), jnp.float32)
    dma = lambda n: pltpu.SemaphoreType.DMA((n,))
    out = pl.pallas_call(
        kernel,
        out_shape=jax.ShapeDtypeStruct((ROWS, 128, 128), jnp.float32),
        in_specs=[
            pl.BlockSpec(memory_space=pltpu.VMEM),
            pl.BlockSpec(memory_space=pl.ANY),
            pl.BlockSpec(memory_space=pl.ANY),
        ],
        out_specs=pl.BlockSpec(memory_space=pltpu.VMEM),
        scratch_shapes=[blocks(15) for _ in range(NZ)] + [
            blocks(2 * NX * ROWS * SLOTS),
            blocks(2 * KEPT * ROWS),
            pltpu.VMEM((2, 128, KEPT * 128), jnp.float32),
            blocks(4 * ROWS),
            blocks(ROWS),
            blocks(2 * ROWS),
            pltpu.VMEM((8, 8, 128), jnp.int32),
            pltpu.VMEM((8, 8, 128), jnp.int32),
            pltpu.VMEM((2, 8, 128), jnp.int32),
            pltpu.SMEM((2, 8, 128), jnp.int32),
            dma(2), pltpu.SemaphoreType.DMA,
            dma(8), dma(8), dma(8), dma(8),
            dma(16), dma(16), dma(16), dma(16),
            pltpu.SemaphoreType.DMA, pltpu.SemaphoreType.DMA,
            dma(6), dma(6), dma(4), dma(4),
            dma(4), dma(4), dma(6), dma(6),
        ],
        compiler_params=pltpu.CompilerParams(
            collective_id=0, has_side_effects=True, vmem_limit_bytes=48 * 1024 * 1024
        ),
        cost_estimate=pl.CostEstimate(flops=2 * 10 ** 9, bytes_accessed=3 * 10 ** 6, transcendentals=0),
    )(meta, a, b)
    return out.reshape(ROWS, 1, 1, 128, 128)


def solution(mesh):
    placed = (
        P("col", "row", None, None),
        P("col", "row", None),
        P("col", "row"),
        P(("col", "rep"), "row", None, None, None),
        P(("col", "rep"), "row", None),
        P("col", "row", None),
    )
    return jax.shard_map(
        local,
        mesh=mesh,
        in_specs=placed,
        out_specs=P("col", "row", "rep", None, None),
        check_vma=False,
    )
```

time: 352 us -> 113 us (0.32)
  waiting for transfers between devices: 236 us -> 0 us
  Pallas kernels: 0 us -> 106 us
  blocking collectives: 38.9 us -> 0 us
  local copies, waits for them, and re-layouts: 32.2 us -> 5.2 us
  other arithmetic: 17.5 us -> 1.39 us
  matrix products: 13.4 us -> 0 us
  between operations: 13.3 us -> 0.03 us
    all_gather x2 -> x0, waiting for transfers between devices: 180 us -> none  [the longest x1 169 us: local(): lax.all_gather(b_vals, 'col', axis=0, tiled=True)]
    pallas_call x0 -> x1, Pallas kernels: none -> 106 us  [local(): pl.pallas_call(kernel, out_shape=jax.ShapeDtypeStruct((ROWS, 128, 128), j...]
    psum x1 -> x0, waiting for transfers between devices: 54.4 us -> none  [local(): summed = lax.psum(partial_value, 'rep')]
    all_gather x2 -> x0, blocking collectives: 38.9 us -> none  [the longest x1 29.7 us: local(): lax.all_gather(b_cols, 'col', axis=0, tiled=True)]
    gather x11 -> x0, local copies, waits for them, and re-layouts: 16.1 us -> none  [the longest x1 9.05 us: add_piece(): b_blocks = piece_vals[local_rows, 0]]
    dot_general x1 -> x0, matrix products: 13.4 us -> none  [add_products(): jnp.einsum('xab,xtbc->xtac', flat_blocks[picked], b_blocks, precision=lax...]
    scatter-add x1 -> x0, other arithmetic: 12.9 us -> none  [add_products(): return totals.at[targets.reshape(-1)].add(flat_products)]
    reshape x3, local copies, waits for them, and re-layouts: 8.38 us -> 0.24 us  [the longest x1 0.08 us: local(): codes = (a_group[:, :, 0] * 8 + a_offset + 1).reshape(-1)]
  transfers between devices with their start and end apart: 3 -> 0, of which waited for: 3 -> 0; matrix products, arithmetic and copies ran while one was open for 5% -> 0% of each run, Pallas kernels for 0% -> 0%
where the time goes in v1:
time: 113 us
  Pallas kernels  106 us (94%)
  local copies, waits for them, and re-layouts  5.2 us (5%)
  other arithmetic  1.39 us (1%)
    pallas_call x1, Pallas kernels, local(): pl.pallas_call(kernel, out_shape=jax.ShapeDtypeStruct((ROWS, 128, 128), j...  106 us
    unnamed x7, local copies, waits for them, and re-layouts  4.75 us

profile of v1, /device:TPU:1, one launch (start us, length us, event | category | flops | bytes accessed | tf_op | source)
XLA Modules:
  0.0 112.9 jit_solution(12149889520963586559)
XLA Ops:
  0.0 0.7 broadcast_multiply_fusion
  0.7 0.7 fusion
  1.4 0.1 copy.11
  1.5 0.1 reshape.68
  1.6 0.1 tile.10
  1.7 0.8 copy.12
  2.4 0.1 reshape.69
  2.5 0.8 copy.13
  3.3 0.1 reshape.70
  3.4 0.0 copy-start
  3.4 1.3 %copy-done = f32[6,3,128,128]{3,2,1,0:T(8,128)S(1)} copy-done((f32[6,3,128,128]{3,2,1,0:T(8,128)S(1)}, f32[6,3,128,128]{3,2,1,0:T(8,128)}, u32[]{:S(2)}) %copy-start) | copy-done | bytes 1179672
  4.7 0.0 copy-start.1
  4.7 1.2 %copy-done.1 = f32[5,1,3,128,128]{4,3,2,1,0:T(8,128)S(1)} copy-done((f32[5,1,3,128,128]{4,3,2,1,0:T(8,128)S(1)}, f32[5,1,3,128,128]{4,3,2,1,0:T(8,128)}, u32[]{:S(2)}) %copy-start.1) | copy-done | bytes 983064
  5.9 106.2 %shard_map.64 = f32[6,128,128]{2,1,0:T(8,128)S(1)} custom-call(s32[8,128]{1,0:T(8,128)S(1)} %pad.19.meta_ref, f32[18,128,128]{2,1,0:T(8,128)S(1)} %bitcast.18, f32[15,128,128]{2,1,0:T(8,128)S(1)} %bitcast.19), custom_call_target="tpu_custom_call" | custom-call | flops 2000000000 | bytes 3000000 | tf_op jit(solution)/shard_map/pallas_call | solution.py:346
  112.1 0.7 copy.18
  (6 shorter events, 0.0 us)
Async XLA Ops:
  3.4 1.3 %copy-start = (f32[6,3,128,128]{3,2,1,0:T(8,128)S(1)}, f32[6,3,128,128]{3,2,1,0:T(8,128)}, u32[]{:S(2)}) copy-start(f32[6,3,128,128]{3,2,1,0:T(8,128)} %param.6) | copy-start | bytes 3538948
  4.7 1.2 %copy-start.1 = (f32[5,1,3,128,128]{4,3,2,1,0:T(8,128)S(1)}, f32[5,1,3,128,128]{4,3,2,1,0:T(8,128)}, u32[]{:S(2)}) copy-start(f32[5,1,3,128,128]{4,3,2,1,0:T(8,128)} %param.9) | copy-start | bytes 2949124

commit v2 on v1

v2 whole, which is shorter than its diff:
```python
import functools
import jax
import jax.numpy as jnp
from jax import lax
from jax.experimental import pallas as pl
from jax.experimental.pallas import tpu as pltpu
from jax.sharding import PartitionSpec as P

NZ = 8
NX = 4
PIECES = ((0, 8), (8, 15))
ROWS = 6
SLOTS = 3
KEPT = 4
TERMS = 3
KPG = 5
BLOCKS = KPG * TERMS
SPAN = ROWS * SLOTS
CUT = SPAN // 2
MID = ROWS // 2


def kernel(
    group_ref, offset_ref, b_cols_ref, c_cols_ref, a_ref, b_ref, out_ref,
    *scratch,
):
    bufs = (scratch[:NZ], scratch[NZ:2 * NZ])
    (
        b_own, a_all, acc, prod, core_in, packed, far_in, near_in,
        meta, meta_a, meta_b, table_v, table_s,
        loc_sem, tab_sem,
        ma_send, ma_recv, mb_send, mb_recv,
        bp_send, bp_recv, bm_send, bm_recv,
        y_send, y_recv, x_send, x_recv, t_send, t_recv,
        c_send, c_recv, r_send, r_recv,
    ) = scratch[2 * NZ:]
    x = lax.axis_index("row")
    col = lax.axis_index("col")
    rep = lax.axis_index("rep")
    z, y_lo = col % NZ, col // NZ
    core, y_hi = rep % 2, rep // 2
    y = y_hi * 2 + y_lo

    def at(x_, y_, z_, core_):
        return (x_, (y_ % 2) * NZ + z_, (y_ // 2) * 2 + core_)

    def z_at(step):
        return at(x, y, (z + step) % NZ, core)

    def x_at(step):
        return at((x + step) % NX, y, z, core)

    def y_at(step):
        return at(x, (y + step) % 4, z, core)

    def pair_at(fy, rx):
        return at((x + rx) % NX, y_hi * 2 + (y_lo + fy) % 2, z, core)

    sibling = at(x, y, z, 1 - core)
    other_y = at(x, (y + 3 - 2 * y_lo) % 4, z, core)

    def copy(src, dst, send, recv, device):
        return pltpu.make_async_remote_copy(
            src_ref=src, dst_ref=dst, send_sem=send, recv_sem=recv,
            device_id=device, device_id_type=pl.DeviceIdType.MESH,
        )

    pairs = [(fy, rx) for fy in range(2) for rx in range(NX) if (fy, rx) != (0, 0)]
    peers = [z_at(r) for r in range(1, NZ)] + [pair_at(*p) for p in pairs] + [other_y, sibling]
    barrier = pltpu.get_barrier_semaphore()
    for peer in peers:
        pl.semaphore_signal(barrier, inc=1, device_id=peer, device_id_type=pl.DeviceIdType.MESH)

    own_b = pltpu.make_async_copy(b_ref, b_own, loc_sem.at[0])
    own_b.start()
    own_a = pltpu.make_async_copy(a_ref, a_all.at[pl.ds(0, SPAN)], loc_sem.at[1])

    @pl.when(core == 0)
    def _():
        own_a.start()

    lane = lax.broadcasted_iota(jnp.int32, (8, 128), 1)
    line = lax.broadcasted_iota(jnp.int32, (8, 128), 0)
    spot = line * 128 + lane
    mine = jnp.zeros((8, 128), jnp.int32)
    for i in range(ROWS):
        for s in range(SLOTS):
            code = group_ref[s, 0, i] * 8 + offset_ref[s, i] + 1
            mine = jnp.where(spot == x * 32 + i * SLOTS + s, code, mine)
        for q in range(KEPT):
            mine = jnp.where(spot == 256 + i * KEPT + q, c_cols_ref[q, i], mine)
    for o in range(KPG):
        for t in range(TERMS):
            mine = jnp.where(spot == 128 + o * TERMS + t, b_cols_ref[t, 0, o], mine)
    meta[...] = mine
    meta_b[0] = mine
    meta_a[0] = mine

    left = lax.broadcasted_iota(jnp.int32, (64, 128), 1) < 64

    def to_halves(block):
        top, bottom = block[:64], block[64:]
        return (
            jnp.where(left, top, pltpu.roll(bottom, 64, 1)),
            jnp.where(left, pltpu.roll(top, 64, 1), bottom),
        )

    own_b.wait()

    def pack(n, carry):
        bufs[0][0][n], bufs[1][0][n] = to_halves(b_own[n])
        return carry

    lax.fori_loop(0, BLOCKS, pack, 0)
    pl.semaphore_wait(barrier, len(peers))

    sent = []

    def go(c):
        c.start()
        sent.append(c)
        return c

    hops = {}

    def hop(h, sign, k, n):
        sems = (bp_send, bp_recv) if sign > 0 else (bm_send, bm_recv)
        lo, hi = PIECES[n if sign > 0 else 1 - n]
        index = h * 8 + k * 2 + n
        hops[h, sign, k, n] = go(copy(
            bufs[h][(-sign * k) % NZ].at[pl.ds(lo, hi - lo)],
            bufs[h][(-sign * (k + 1)) % NZ].at[pl.ds(lo, hi - lo)],
            sems[0].at[index], sems[1].at[index], z_at(sign),
        ))

    def begin(h):
        for n in range(2):
            hop(h, 1, 0, n)
            hop(h, -1, 0, n)

    def forward(h, k, n, on=True):
        for sign in (1, -1):
            hops[h, sign, k - 1, n].wait_recv()
            if on:
                hop(h, sign, k, n)

    begin(0)
    cross_a = [
        copy(a_ref.at[pl.ds(0, CUT)], a_all.at[pl.ds(0, CUT)], y_send.at[0], y_recv.at[0], pair_at(1, 0)),
        copy(a_ref.at[pl.ds(CUT, SPAN - CUT)], a_all.at[pl.ds(CUT, SPAN - CUT)], y_send.at[1], y_recv.at[1], other_y),
    ]

    def a_part(slot, lo, hi):
        return a_all.at[pl.ds(slot * SPAN + lo, hi - lo)]

    xs = [
        copy(a_part(0, 0, CUT), a_part(1, 0, CUT), x_send.at[0], x_recv.at[0], x_at(1)),
        copy(a_part(0, CUT, SPAN), a_part(2, CUT, SPAN), x_send.at[1], x_recv.at[1], x_at(NX - 1)),
        copy(a_part(0, CUT, SPAN), a_part(1, CUT, SPAN), x_send.at[2], x_recv.at[2], x_at(1)),
        copy(a_part(0, 0, CUT), a_part(2, 0, CUT), x_send.at[3], x_recv.at[3], x_at(NX - 1)),
        copy(a_part(1, 0, CUT), a_part(3, 0, CUT), x_send.at[4], x_recv.at[4], x_at(1)),
        copy(a_part(2, CUT, SPAN), a_part(3, CUT, SPAN), x_send.at[5], x_recv.at[5], x_at(NX - 1)),
    ]
    ts = [
        copy(a_part(k, 0, SPAN), a_part(NX + k, 0, SPAN), t_send.at[k], t_recv.at[k], sibling)
        for k in range(NX)
    ]

    @pl.when(core == 1)
    def _():
        for c in cross_a:
            c.start()

    @pl.when(core == 0)
    def _():
        own_a.wait()
        for c in xs[:4]:
            c.start()

    to_z = [go(copy(meta, meta_b.at[r], mb_send.at[r], mb_recv.at[r], z_at(r))) for r in range(1, NZ)]
    to_pair = [
        go(copy(meta, meta_a.at[fy * NX + rx], ma_send.at[fy * NX + rx], ma_recv.at[fy * NX + rx], pair_at(fy, rx)))
        for fy, rx in pairs
    ]

    forward(0, 1, 0)

    @pl.when(core == 1)
    def _():
        for c in cross_a:
            c.wait_recv()
        for c in xs[:4]:
            c.start()

    sent.extend(xs[:4])
    go(ts[0])
    forward(0, 1, 1)

    for c in to_z + to_pair:
        c.wait_recv()
    b_cols = jnp.concatenate([meta_b[(NZ - d) % NZ, 1:2, :] for d in range(NZ)], axis=0)
    away = (lane // 32 - x + NX) % NX
    inside = lane % 32
    place = jnp.where(away == 0, 0, jnp.where(away == 3, 1, jnp.where(away == 1, 2, 3))) * SPAN + inside
    owner = jnp.zeros((8, 128), jnp.int32)
    for m in range(1, ROWS):
        owner = owner + jnp.where(inside >= SLOTS * m, 1, 0)
    group = (y_lo * NZ + (line + z) % NZ) * 4 + rep

    def pick(where, value):
        return jnp.sum(jnp.where(where, value, 0), axis=1, keepdims=True)

    for s in range(2):
        flip = (core + s) % 2
        base = flip * NX
        codes = meta_a[base, 0:1, :]
        for rx in range(1, NX):
            codes = codes + meta_a[base + rx, 0:1, :]
        codes = jnp.broadcast_to(codes, (8, 128)) - 1
        wanted = jnp.broadcast_to(meta_a[base, 2:3, :], (8, 128))
        match = (codes >= 0) & (codes // 8 == group)
        first = jnp.min(jnp.where(match, lane, 1000), axis=1, keepdims=True)
        last = jnp.max(jnp.where(match, lane, -1), axis=1, keepdims=True)
        result = jnp.zeros((8, 128), jnp.int32)
        for k in range(2):
            chosen = match & (lane == first) if k == 0 else match & (lane == last) & (lane != first)
            exists = pick(chosen, 1)
            index = pick(chosen, place + s * NX * SPAN)
            offset = pick(chosen, codes % 8)
            row = pick(chosen, owner)
            result = result + jnp.where(lane == k * 32, index, 0)
            result = result + jnp.where(lane == k * 32 + 1, offset * TERMS, 0)
            result = result + jnp.where(lane == k * 32 + 2, row, 0)
            kept = [pick(lane == row * KEPT + q, wanted) for q in range(KEPT)]
            for t in range(TERMS):
                target = pick(lane == offset * TERMS + t, b_cols)
                for q in range(KEPT):
                    hit = jnp.where((target == kept[q]) & (exists > 0), 1, 0)
                    result = result + jnp.where(lane == k * 32 + 8 + t * KEPT + q, hit, 0)
        table_v[s] = result
    to_scalar = pltpu.make_async_copy(table_v, table_s, tab_sem)
    to_scalar.start()
    to_scalar.wait()

    forward(0, 2, 0)
    forward(0, 2, 1)
    xs[0].wait_recv()
    go(xs[4])
    xs[1].wait_recv()
    go(xs[5])
    forward(0, 3, 0)
    begin(1)
    forward(0, 3, 1, False)
    xs[2].wait_recv()
    go(ts[1])
    xs[3].wait_recv()
    go(ts[2])

    def multiply(h, d, stream):
        buf = bufs[h][d]
        base = (h * 2 + (y_lo + core + stream) % 2) * 2 * ROWS
        for k in range(2):
            a = a_all[table_s[stream, d, k * 32]]
            offset = table_s[stream, d, k * 32 + 1]
            terms = [buf[offset + t] for t in range(TERMS)]
            chosen = []
            for q in range(KEPT):
                weights = [table_s[stream, d, k * 32 + 8 + t * KEPT + q].astype(jnp.float32) for t in range(TERMS)]
                chosen.append(weights[0] * terms[0] + weights[1] * terms[1] + weights[2] * terms[2])
            turned = [pltpu.roll(c, 64, 1) for c in chosen]
            b = jnp.concatenate([
                jnp.concatenate([jnp.where(left, chosen[g], turned[g + 2]) for g in range(2)], axis=1),
                jnp.concatenate([jnp.where(left, turned[g], chosen[g + 2]) for g in range(2)], axis=1),
            ], axis=0)
            a_hi = a.astype(jnp.bfloat16)
            a_lo = (a - a_hi.astype(jnp.float32)).astype(jnp.bfloat16)
            b_hi = b.astype(jnp.bfloat16)
            b_lo = (b - b_hi.astype(jnp.float32)).astype(jnp.bfloat16)
            dot = functools.partial(jnp.dot, preferred_element_type=jnp.float32)
            prod[k] = dot(a_hi, b_hi) + (dot(a_hi, b_lo) + dot(a_lo, b_hi))
        rows = [table_s[stream, d, k * 32 + 2] for k in range(2)]

        def update(i, carry):
            w0 = jnp.where(rows[0] == i, 1.0, 0.0).astype(jnp.float32)
            w1 = jnp.where(rows[1] == i, 1.0, 0.0).astype(jnp.float32)
            for g in range(2):
                cols = pl.ds(g * 128, 128)
                term = w0 * prod[0, :, cols] + w1 * prod[1, :, cols]
                where = base + g * ROWS + i
                acc[where] = term if d == 0 else acc[where] + term
            return carry

        lax.fori_loop(0, ROWS, update, 0)

    def multiply_all(h, *ds):
        for d in ds:
            def both(stream, carry, d=d):
                multiply(h, d, stream)
                return carry

            lax.fori_loop(0, 2, both, 0)

    cores, far, near = {}, {}, {}

    def to_sibling(h, e):
        start = (h * 4 + ((y_lo + e) % 2) * 2 + 1 - core) * ROWS
        cores[h, e] = go(copy(
            acc.at[pl.ds(start, ROWS)], core_in.at[pl.ds((h * 2 + e) * ROWS, ROWS)],
            c_send.at[h * 2 + e], c_recv.at[h * 2 + e], sibling,
        ))

    def fold(h, e):
        cores[h, e].wait_recv()
        lo = (y_lo + e) % 2
        start = (h * 4 + lo * 2 + core) * ROWS
        for i in range(ROWS):
            halves = to_halves(core_in[(h * 2 + e) * ROWS + i] + acc[start + i])
            packed[(h * 4 + lo) * ROWS + i] = halves[0]
            packed[(h * 4 + 2 + lo) * ROWS + i] = halves[1]

    def place_of(h, step):
        return (h * 4 + (y + step) % 4) * ROWS

    def send_y(h, step, lo, dst, dst_lo, index, way):
        return go(copy(
            packed.at[pl.ds(place_of(h, step) + lo, MID)], dst.at[pl.ds(dst_lo, MID)],
            r_send.at[h * 6 + index], r_recv.at[h * 6 + index], y_at(way),
        ))

    def fold_far(h):
        fold(h, 0)
        far[h] = [
            send_y(h, 2, 0, far_in, h * ROWS, 0, 1),
            send_y(h, 2, MID, far_in, h * ROWS + MID, 1, 3),
        ]

    def fold_near(h):
        fold(h, 1)
        near[h] = [
            send_y(h, 1, MID, near_in, h * 2 * ROWS + MID, 2, 1),
            send_y(h, 3, 0, near_in, h * 2 * ROWS + ROWS, 3, 3),
        ]

    def add_far(h):
        for way, lo in ((1, 0), (3, MID)):
            far[h][lo // MID].wait_recv()
            for i in range(lo, lo + MID):
                where = place_of(h, way) + i
                packed[where] = packed[where] + far_in[h * ROWS + i]
            near[h].append(send_y(
                h, way, lo, near_in, h * 2 * ROWS + (0 if way == 1 else ROWS) + lo, 4 + lo // MID, way,
            ))

    def finish(h):
        for c in near[h]:
            c.wait_recv()
        for i in range(ROWS):
            where = place_of(h, 0) + i
            base = h * 2 * ROWS + i
            packed[where] = packed[where] + near_in[base] + near_in[base + ROWS]

    forward(1, 1, 0)
    xs[4].wait_recv()
    xs[5].wait_recv()
    go(ts[3])
    for n in range(1):
        hops[0, 1, 3, n].wait_recv()
        hops[0, -1, 3, n].wait_recv()
    forward(1, 1, 1)
    for c in ts:
        c.wait_recv()
    multiply_all(0, 0, 1, 7)
    forward(1, 2, 0)
    multiply_all(0, 2, 6, 3, 5)
    forward(1, 2, 1)
    multiply_all(0, 4)
    to_sibling(0, 0)
    to_sibling(0, 1)
    multiply_all(1, 0)
    fold_far(0)
    fold_near(0)
    multiply_all(1, 1, 7)
    forward(1, 3, 0)
    multiply_all(1, 2, 6)
    add_far(0)
    forward(1, 3, 1, False)
    multiply_all(1, 3, 5)
    finish(0)
    hops[1, 1, 3, 0].wait_recv()
    hops[1, -1, 3, 0].wait_recv()
    multiply(1, 4, core)
    to_sibling(1, 0)
    multiply(1, 4, 1 - core)
    to_sibling(1, 1)
    fold_far(1)
    fold_near(1)
    add_far(1)
    finish(1)
    for i in range(ROWS):
        first, second = packed[place_of(0, 0) + i], packed[place_of(1, 0) + i]
        out_ref[i, pl.ds(0, 64)] = jnp.where(left, first, pltpu.roll(second, 64, 1))
        out_ref[i, pl.ds(64, 64)] = jnp.where(left, pltpu.roll(first, 64, 1), second)

    for c in sent:
        c.wait_send()

    @pl.when(core == 1)
    def _():
        for c in cross_a:
            c.wait_send()


def local(a_vals, a_group, a_offset, b_vals, b_cols, c_cols):
    a = a_vals.reshape(-1, 128, 128)
    b = b_vals.reshape(-1, 128, 128)
    blocks = lambda n: pltpu.VMEM((n, 128, 128), jnp.float32)
    thin = lambda n: pltpu.VMEM((n, 64, 128), jnp.float32)
    dma = lambda n: pltpu.SemaphoreType.DMA((n,))
    out = pl.pallas_call(
        kernel,
        out_shape=jax.ShapeDtypeStruct((ROWS, 128, 128), jnp.float32),
        in_specs=[pl.BlockSpec(memory_space=pltpu.SMEM)] * 4 + [pl.BlockSpec(memory_space=pltpu.HBM)] * 2,
        out_specs=pl.BlockSpec(memory_space=pltpu.VMEM),
        scratch_shapes=[thin(BLOCKS) for _ in range(2 * NZ)] + [
            blocks(BLOCKS),
            blocks(2 * NX * SPAN),
            blocks(2 * 4 * ROWS),
            pltpu.VMEM((2, 128, 256), jnp.float32),
            blocks(4 * ROWS),
            thin(2 * 4 * ROWS),
            thin(2 * ROWS),
            thin(4 * ROWS),
            pltpu.VMEM((8, 128), jnp.int32),
            pltpu.VMEM((8, 8, 128), jnp.int32),
            pltpu.VMEM((8, 8, 128), jnp.int32),
            pltpu.VMEM((2, 8, 128), jnp.int32),
            pltpu.SMEM((2, 8, 128), jnp.int32),
            dma(2), pltpu.SemaphoreType.DMA,
            dma(8), dma(8), dma(8), dma(8),
            dma(16), dma(16), dma(16), dma(16),
            dma(2), dma(2), dma(6), dma(6), dma(4), dma(4),
            dma(4), dma(4), dma(12), dma(12),
        ],
        compiler_params=pltpu.CompilerParams(
            collective_id=0, has_side_effects=True, vmem_limit_bytes=62 * 1024 * 1024
        ),
        cost_estimate=pl.CostEstimate(flops=2 * 10 ** 9, bytes_accessed=3 * 10 ** 6, transcendentals=0),
    )(
        a_group.transpose(1, 2, 0), a_offset.T, b_cols.transpose(2, 1, 0), c_cols[:, 0].T, a, b,
    )
    return out.reshape(ROWS, 1, 1, 128, 128)


def solution(mesh):
    placed = (
        P("col", "row", None, None),
        P("col", "row", None),
        P("col", "row"),
        P(("col", "rep"), "row", None, None, None),
        P(("col", "rep"), "row", None),
        P("col", "row", None),
    )
    return jax.shard_map(
        local,
        mesh=mesh,
        in_specs=placed,
        out_specs=P("col", "row", "rep", None, None),
        check_vma=False,
    )
```

time: 113 us -> 103 us (0.912)
  Pallas kernels: 106 us -> 101 us
  local copies, waits for them, and re-layouts: 5.2 us -> 1.77 us
  other arithmetic: 1.39 us -> 0 us
    pallas_call x1, Pallas kernels: 106 us -> 101 us  [local(): pl.pallas_call(kernel, out_shape=jax.ShapeDtypeStruct((ROWS, 128, 128), j...]
    unnamed x7 -> x1, local copies, waits for them, and re-layouts: 4.75 us -> 1.77 us
where the time goes in v2:
time: 103 us
  Pallas kernels  101 us (98%)
  local copies, waits for them, and re-layouts  1.77 us (2%)
    pallas_call x1, Pallas kernels, local(): pl.pallas_call(kernel, out_shape=jax.ShapeDtypeStruct((ROWS, 128, 128), j...  101 us

profile of v2, /device:TPU:1, one launch (start us, length us, event | category | flops | bytes accessed | tf_op | source)
XLA Modules:
  0.0 103.0 jit_solution(14614909370320052467)
XLA Ops:
  0.0 101.2 %shard_map.64 = f32[6,128,128]{2,1,0:T(8,128)} custom-call(s32[3,1,6]{2,1,0:T(1,128)} %bitcast.16, s32[3,6]{1,0:T(4,128)} %bitcast.14, s32[3,1,5]{2,1,0:T(1,128)} %bitcast.17, s32[4,6]{1,0:T(4,128)} %bitcast.15, f32[18,128,128]{2,1,0:T(8,128)} %bitcast.12, f32[15,128,128]{2,1,0:T(8,128)} %bitcast.13), custom_call_target="tpu_custom_call" | custom-call | flops 2000000000 | bytes 3000000 | tf_op jit(solution)/shard_map/pallas_call | solution.py:419
  101.3 1.8 %copy.9 = f32[6,1,1,128,128]{4,3,2,1,0:T(8,128)} copy(f32[6,1,1,128,128]{4,3,2,1,0:T(8,128)} %bitcast.11) | data formatting | bytes 786432

commit v3 on v2

--- a/solution.py
+++ b/solution.py
@@ -8,7 +8,8 @@
 
 NZ = 8
 NX = 4
-PIECES = ((0, 8), (8, 15))
+HALF_CUT = 8
+QUARTER_CUT = 7
 ROWS = 6
 SLOTS = 3
 KEPT = 4
@@ -24,16 +25,21 @@
     group_ref, offset_ref, b_cols_ref, c_cols_ref, a_ref, b_ref, out_ref,
     *scratch,
 ):
-    bufs = (scratch[:NZ], scratch[NZ:2 * NZ])
+    bufs = (scratch[:NZ], scratch[NZ:2 * NZ], scratch[2 * NZ:3 * NZ])
     (
-        b_own, a_all, acc, prod, core_in, packed, far_in, near_in,
+        b_own, a_all, prod, quarter_acc, own_core, core_in_0, core_in_1, core_in_2, acc,
+        packed_0, packed_1, packed_2, far_0, far_1, far_2, near_0, near_1, near_2,
         meta, meta_a, meta_b, table_v, table_s,
         loc_sem, tab_sem,
         ma_send, ma_recv, mb_send, mb_recv,
         bp_send, bp_recv, bm_send, bm_recv,
         y_send, y_recv, x_send, x_recv, t_send, t_recv,
         c_send, c_recv, r_send, r_recv,
-    ) = scratch[2 * NZ:]
+    ) = scratch[3 * NZ:]
+    core_in = (core_in_0, core_in_1, core_in_2)
+    packed = (packed_0, packed_1, packed_2)
+    far_in = (far_0, far_1, far_2)
+    near_in = (near_0, near_1, near_2)
     x = lax.axis_index("row")
     col = lax.axis_index("col")
     rep = lax.axis_index("rep")
@@ -105,10 +111,21 @@
             jnp.where(left, pltpu.roll(top, 64, 1), bottom),
         )
 
+    even = lax.broadcasted_iota(jnp.int32, (32, 128), 1) % 64 < 32
+    left_thin = left[:32]
+
+    def to_quarters(half):
+        top, bottom = half[:32], half[32:]
+        return (
+            jnp.where(even, top, pltpu.roll(bottom, 32, 1)),
+            jnp.where(even, pltpu.roll(top, 96, 1), bottom),
+        )
+
     own_b.wait()
 
     def pack(n, carry):
-        bufs[0][0][n], bufs[1][0][n] = to_halves(b_own[n])
+        bufs[0][0][n], half = to_halves(b_own[n])
+        bufs[1][0][n], bufs[2][0][n] = to_quarters(half)
         return carry
 
     lax.fori_loop(0, BLOCKS, pack, 0)
@@ -125,7 +142,8 @@
 
     def hop(h, sign, k, n):
         sems = (bp_send, bp_recv) if sign > 0 else (bm_send, bm_recv)
-        lo, hi = PIECES[n if sign > 0 else 1 - n]
+        split = HALF_CUT if h == 0 else QUARTER_CUT
+        lo, hi = (0, split) if (n == 0) == (sign > 0) else (split, BLOCKS)
         index = h * 8 + k * 2 + n
         hops[h, sign, k, n] = go(copy(
             bufs[h][(-sign * k) % NZ].at[pl.ds(lo, hi - lo)],
@@ -145,6 +163,7 @@
                 hop(h, sign, k, n)
 
     begin(0)
+    begin(1)
     cross_a = [
         copy(a_ref.at[pl.ds(0, CUT)], a_all.at[pl.ds(0, CUT)], y_send.at[0], y_recv.at[0], pair_at(1, 0)),
         copy(a_ref.at[pl.ds(CUT, SPAN - CUT)], a_all.at[pl.ds(CUT, SPAN - CUT)], y_send.at[1], y_recv.at[1], other_y),
@@ -195,6 +214,8 @@
     sent.extend(xs[:4])
     go(ts[0])
     forward(0, 1, 1)
+    forward(1, 1, 0)
+    forward(1, 1, 1)
 
     for c in to_z + to_pair:
         c.wait_recv()
@@ -244,22 +265,27 @@
 
     forward(0, 2, 0)
     forward(0, 2, 1)
+    forward(1, 2, 0)
+    forward(1, 2, 1)
     xs[0].wait_recv()
     go(xs[4])
     xs[1].wait_recv()
     go(xs[5])
     forward(0, 3, 0)
-    begin(1)
+    begin(2)
     forward(0, 3, 1, False)
     xs[2].wait_recv()
     go(ts[1])
     xs[3].wait_recv()
     go(ts[2])
 
-    def multiply(h, d, stream):
-        buf = bufs[h][d]
-        base = (h * 2 + (y_lo + core + stream) % 2) * 2 * ROWS
-        for k in range(2):
+    def multiply(h, ds, stream):
+        lo = (y_lo + core + stream) % 2
+        base = lo * 2 * ROWS if h == 0 else ((h - 1) * 2 + lo) * ROWS
+        into = acc if h == 0 else quarter_acc
+        slots = [(d, k) for d in ds for k in range(2)]
+        for d, k in slots:
+            buf = bufs[h][d]
             a = a_all[table_s[stream, d, k * 32]]
             offset = table_s[stream, d, k * 32 + 1]
             terms = [buf[offset + t] for t in range(TERMS)]
@@ -268,77 +294,100 @@
                 weights = [table_s[stream, d, k * 32 + 8 + t * KEPT + q].astype(jnp.float32) for t in range(TERMS)]
                 chosen.append(weights[0] * terms[0] + weights[1] * terms[1] + weights[2] * terms[2])
             turned = [pltpu.roll(c, 64, 1) for c in chosen]
-            b = jnp.concatenate([
-                jnp.concatenate([jnp.where(left, chosen[g], turned[g + 2]) for g in range(2)], axis=1),
-                jnp.concatenate([jnp.where(left, turned[g], chosen[g + 2]) for g in range(2)], axis=1),
-            ], axis=0)
+            if h == 0:
+                b = jnp.concatenate([
+                    jnp.concatenate([jnp.where(left, chosen[g], turned[g + 2]) for g in range(2)], axis=1),
+                    jnp.concatenate([jnp.where(left, turned[g], chosen[g + 2]) for g in range(2)], axis=1),
+                ], axis=0)
+            else:
+                parts = []
+                for upper in (True, False):
+                    pair = [
+                        jnp.where(left_thin, chosen[g], turned[g + 1]) if upper
+                        else jnp.where(left_thin, turned[g], chosen[g + 1])
+                        for g in (0, 2)
+                    ]
+                    parts.append(jnp.where(even, pair[0], pltpu.roll(pair[1], 32, 1)))
+                    parts.append(jnp.where(even, pltpu.roll(pair[0], 96, 1), pair[1]))
+                b = jnp.concatenate(parts, axis=0)
             a_hi = a.astype(jnp.bfloat16)
             a_lo = (a - a_hi.astype(jnp.float32)).astype(jnp.bfloat16)
             b_hi = b.astype(jnp.bfloat16)
             b_lo = (b - b_hi.astype(jnp.float32)).astype(jnp.bfloat16)
             dot = functools.partial(jnp.dot, preferred_element_type=jnp.float32)
-            prod[k] = dot(a_hi, b_hi) + (dot(a_hi, b_lo) + dot(a_lo, b_hi))
-        rows = [table_s[stream, d, k * 32 + 2] for k in range(2)]
+            prod[slots.index((d, k)), :, pl.ds(0, b.shape[1])] = dot(a_hi, b_hi) + (dot(a_hi, b_lo) + dot(a_lo, b_hi))
+        rows = [table_s[stream, d, k * 32 + 2] for d, k in slots]
 
         def update(i, carry):
-            w0 = jnp.where(rows[0] == i, 1.0, 0.0).astype(jnp.float32)
-            w1 = jnp.where(rows[1] == i, 1.0, 0.0).astype(jnp.float32)
-            for g in range(2):
-                cols = pl.ds(g * 128, 128)
-                term = w0 * prod[0, :, cols] + w1 * prod[1, :, cols]
+            weights = [jnp.where(row == i, 1.0, 0.0).astype(jnp.float32) for row in rows]
+            for g in range(2 if h == 0 else 1):
                 where = base + g * ROWS + i
-                acc[where] = term if d == 0 else acc[where] + term
+                total = None if 0 in ds else into[where]
+                for n, weight in enumerate(weights):
+                    term = weight * prod[n, :, pl.ds(g * 128, 128)]
+                    total = term if total is None else total + term
+                into[where] = total
             return carry
 
         lax.fori_loop(0, ROWS, update, 0)
 
     def multiply_all(h, *ds):
-        for d in ds:
-            def both(stream, carry, d=d):
-                multiply(h, d, stream)
-                return carry
-
-            lax.fori_loop(0, 2, both, 0)
+        def both(stream, carry):
+            multiply(h, ds, stream)
+            return carry
+
+        lax.fori_loop(0, 2, both, 0)
 
     cores, far, near = {}, {}, {}
 
     def to_sibling(h, e):
-        start = (h * 4 + ((y_lo + e) % 2) * 2 + 1 - core) * ROWS
+        lo = (y_lo + e) % 2
+        if h == 0:
+            src = acc.at[pl.ds((lo * 2 + 1 - core) * ROWS, ROWS)]
+        else:
+            for i in range(ROWS):
+                halves = to_halves(quarter_acc[((h - 1) * 2 + lo) * ROWS + i])
+                for c in range(2):
+                    own_core[(((h - 1) * 2 + lo) * 2 + c) * ROWS + i] = halves[c]
+            src = own_core.at[pl.ds((((h - 1) * 2 + lo) * 2 + 1 - core) * ROWS, ROWS)]
         cores[h, e] = go(copy(
-            acc.at[pl.ds(start, ROWS)], core_in.at[pl.ds((h * 2 + e) * ROWS, ROWS)],
-            c_send.at[h * 2 + e], c_recv.at[h * 2 + e], sibling,
+            src, core_in[h].at[pl.ds(e * ROWS, ROWS)], c_send.at[h * 2 + e], c_recv.at[h * 2 + e], sibling,
         ))
 
     def fold(h, e):
         cores[h, e].wait_recv()
         lo = (y_lo + e) % 2
-        start = (h * 4 + lo * 2 + core) * ROWS
         for i in range(ROWS):
-            halves = to_halves(core_in[(h * 2 + e) * ROWS + i] + acc[start + i])
-            packed[(h * 4 + lo) * ROWS + i] = halves[0]
-            packed[(h * 4 + 2 + lo) * ROWS + i] = halves[1]
+            if h == 0:
+                pieces = to_halves(core_in[h][e * ROWS + i] + acc[(lo * 2 + core) * ROWS + i])
+            else:
+                pieces = to_quarters(
+                    core_in[h][e * ROWS + i] + own_core[(((h - 1) * 2 + lo) * 2 + core) * ROWS + i]
+                )
+            packed[h][lo * ROWS + i] = pieces[0]
+            packed[h][(2 + lo) * ROWS + i] = pieces[1]
 
     def place_of(h, step):
-        return (h * 4 + (y + step) % 4) * ROWS
+        return ((y + step) % 4) * ROWS
 
     def send_y(h, step, lo, dst, dst_lo, index, way):
         return go(copy(
-            packed.at[pl.ds(place_of(h, step) + lo, MID)], dst.at[pl.ds(dst_lo, MID)],
+            packed[h].at[pl.ds(place_of(h, step) + lo, MID)], dst.at[pl.ds(dst_lo, MID)],
             r_send.at[h * 6 + index], r_recv.at[h * 6 + index], y_at(way),
         ))
 
     def fold_far(h):
         fold(h, 0)
         far[h] = [
-            send_y(h, 2, 0, far_in, h * ROWS, 0, 1),
-            send_y(h, 2, MID, far_in, h * ROWS + MID, 1, 3),
+            send_y(h, 2, 0, far_in[h], 0, 0, 1),
+            send_y(h, 2, MID, far_in[h], MID, 1, 3),
         ]
 
     def fold_near(h):
         fold(h, 1)
         near[h] = [
-            send_y(h, 1, MID, near_in, h * 2 * ROWS + MID, 2, 1),
-            send_y(h, 3, 0, near_in, h * 2 * ROWS + ROWS, 3, 3),
+            send_y(h, 1, MID, near_in[h], MID, 2, 1),
+            send_y(h, 3, 0, near_in[h], ROWS, 3, 3),
         ]
 
     def add_far(h):
@@ -346,9 +395,9 @@
             far[h][lo // MID].wait_recv()
             for i in range(lo, lo + MID):
                 where = place_of(h, way) + i
-                packed[where] = packed[where] + far_in[h * ROWS + i]
+                packed[h][where] = packed[h][where] + far_in[h][i]
             near[h].append(send_y(
-                h, way, lo, near_in, h * 2 * ROWS + (0 if way == 1 else ROWS) + lo, 4 + lo // MID, way,
+                h, way, lo, near_in[h], (0 if way == 1 else ROWS) + lo, 4 + lo // MID, way,
             ))
 
     def finish(h):
@@ -356,48 +405,64 @@
             c.wait_recv()
         for i in range(ROWS):
             where = place_of(h, 0) + i
-            base = h * 2 * ROWS + i
-            packed[where] = packed[where] + near_in[base] + near_in[base + ROWS]
-
-    forward(1, 1, 0)
+            packed[h][where] = packed[h][where] + near_in[h][i] + near_in[h][ROWS + i]
+
+    def last(h):
+        hops[h, 1, 3, 0].wait_recv()
+        hops[h, -1, 3, 0].wait_recv()
+
     xs[4].wait_recv()
     xs[5].wait_recv()
     go(ts[3])
-    for n in range(1):
-        hops[0, 1, 3, n].wait_recv()
-        hops[0, -1, 3, n].wait_recv()
-    forward(1, 1, 1)
+    forward(1, 3, 0)
+    forward(1, 3, 1, False)
     for c in ts:
         c.wait_recv()
     multiply_all(0, 0, 1, 7)
-    forward(1, 2, 0)
-    multiply_all(0, 2, 6, 3, 5)
-    forward(1, 2, 1)
-    multiply_all(0, 4)
+    multiply_all(0, 2, 6)
+    forward(2, 1, 0)
+    multiply_all(1, 0, 1, 7)
+    multiply_all(1, 2, 6)
+    forward(2, 1, 1)
+    last(0)
+    multiply_all(0, 3, 5, 4)
     to_sibling(0, 0)
     to_sibling(0, 1)
-    multiply_all(1, 0)
+    last(1)
+    multiply_all(1, 3, 5, 4)
+    to_sibling(1, 0)
+    to_sibling(1, 1)
+    forward(2, 2, 0)
     fold_far(0)
+    fold_far(1)
     fold_near(0)
-    multiply_all(1, 1, 7)
-    forward(1, 3, 0)
-    multiply_all(1, 2, 6)
+    fold_near(1)
+    forward(2, 2, 1)
+    multiply_all(2, 0, 1, 7)
     add_far(0)
-    forward(1, 3, 1, False)
-    multiply_all(1, 3, 5)
+    add_far(1)
+    forward(2, 3, 0)
+    multiply_all(2, 2, 6)
+    forward(2, 3, 1, False)
+    multiply_all(2, 3, 5)
+    last(2)
+    multiply(2, (4,), core)
+    to_sibling(2, 0)
+    multiply(2, (4,), 1 - core)
+    to_sibling(2, 1)
     finish(0)
-    hops[1, 1, 3, 0].wait_recv()
-    hops[1, -1, 3, 0].wait_recv()
-    multiply(1, 4, core)
-    to_sibling(1, 0)
-    multiply(1, 4, 1 - core)
-    to_sibling(1, 1)
-    fold_far(1)
-    fold_near(1)
-    add_far(1)
     finish(1)
+    fold_far(2)
+    fold_near(2)
+    add_far(2)
+    finish(2)
     for i in range(ROWS):
-        first, second = packed[place_of(0, 0) + i], packed[place_of(1, 0) + i]
+        where = place_of(0, 0) + i
+        first, third, fourth = packed[0][where], packed[1][where], packed[2][where]
+        second = jnp.concatenate([
+            jnp.where(even, third, pltpu.roll(fourth, 32, 1)),
+            jnp.where(even, pltpu.roll(third, 96, 1), fourth),
+        ], axis=0)
         out_ref[i, pl.ds(0, 64)] = jnp.where(left, first, pltpu.roll(second, 64, 1))
         out_ref[i, pl.ds(64, 64)] = jnp.where(left, pltpu.roll(first, 64, 1), second)
 
@@ -415,21 +480,23 @@
     b = b_vals.reshape(-1, 128, 128)
     blocks = lambda n: pltpu.VMEM((n, 128, 128), jnp.float32)
     thin = lambda n: pltpu.VMEM((n, 64, 128), jnp.float32)
+    slim = lambda n: pltpu.VMEM((n, 32, 128), jnp.float32)
     dma = lambda n: pltpu.SemaphoreType.DMA((n,))
     out = pl.pallas_call(
         kernel,
         out_shape=jax.ShapeDtypeStruct((ROWS, 128, 128), jnp.float32),
         in_specs=[pl.BlockSpec(memory_space=pltpu.SMEM)] * 4 + [pl.BlockSpec(memory_space=pltpu.HBM)] * 2,
         out_specs=pl.BlockSpec(memory_space=pltpu.VMEM),
-        scratch_shapes=[thin(BLOCKS) for _ in range(2 * NZ)] + [
+        scratch_shapes=[thin(BLOCKS)] * NZ + [slim(BLOCKS)] * (2 * NZ) + [
             blocks(BLOCKS),
             blocks(2 * NX * SPAN),
-            blocks(2 * 4 * ROWS),
-            pltpu.VMEM((2, 128, 256), jnp.float32),
+            pltpu.VMEM((8, 128, 256), jnp.float32),
+            blocks(4 * ROWS), thin(8 * ROWS),
+            blocks(2 * ROWS), thin(2 * ROWS), thin(2 * ROWS),
             blocks(4 * ROWS),
-            thin(2 * 4 * ROWS),
-            thin(2 * ROWS),
-            thin(4 * ROWS),
+            thin(4 * ROWS), slim(4 * ROWS), slim(4 * ROWS),
+            thin(ROWS), slim(ROWS), slim(ROWS),
+            thin(2 * ROWS), slim(2 * ROWS), slim(2 * ROWS),
             pltpu.VMEM((8, 128), jnp.int32),
             pltpu.VMEM((8, 8, 128), jnp.int32),
             pltpu.VMEM((8, 8, 128), jnp.int32),
@@ -437,9 +504,9 @@
             pltpu.SMEM((2, 8, 128), jnp.int32),
             dma(2), pltpu.SemaphoreType.DMA,
             dma(8), dma(8), dma(8), dma(8),
-            dma(16), dma(16), dma(16), dma(16),
+            dma(24), dma(24), dma(24), dma(24),
             dma(2), dma(2), dma(6), dma(6), dma(4), dma(4),
-            dma(4), dma(4), dma(12), dma(12),
+            dma(6), dma(6), dma(18), dma(18),
         ],
         compiler_params=pltpu.CompilerParams(
             collective_id=0, has_side_effects=True, vmem_limit_bytes=62 * 1024 * 1024

time: 103 us -> 101 us (0.981)
  Pallas kernels: 101 us -> 98.8 us
    pallas_call x1, Pallas kernels: 101 us -> 98.8 us  [local(): pl.pallas_call(kernel, out_shape=jax.ShapeDtypeStruct((ROWS, 128, 128), j...]
where the time goes in v3:
time: 101 us
  Pallas kernels  98.8 us (98%)
  local copies, waits for them, and re-layouts  1.77 us (2%)
    pallas_call x1, Pallas kernels, local(): pl.pallas_call(kernel, out_shape=jax.ShapeDtypeStruct((ROWS, 128, 128), j...  98.8 us

profile of v3, /device:TPU:1, one launch (start us, length us, event | category | flops | bytes accessed | tf_op | source)
XLA Modules:
  0.0 100.6 jit_solution(2659393157557182168)
XLA Ops:
  0.0 98.8 %shard_map.64 = f32[6,128,128]{2,1,0:T(8,128)} custom-call(s32[3,1,6]{2,1,0:T(1,128)} %bitcast.16, s32[3,6]{1,0:T(4,128)} %bitcast.14, s32[3,1,5]{2,1,0:T(1,128)} %bitcast.17, s32[4,6]{1,0:T(4,128)} %bitcast.15, f32[18,128,128]{2,1,0:T(8,128)} %bitcast.12, f32[15,128,128]{2,1,0:T(8,128)} %bitcast.13), custom_call_target="tpu_custom_call" | custom-call | flops 2000000000 | bytes 3000000 | tf_op jit(solution)/shard_map/pallas_call | solution.py:485
  98.8 1.8 %copy.9 = f32[6,1,1,128,128]{4,3,2,1,0:T(8,128)} copy(f32[6,1,1,128,128]{4,3,2,1,0:T(8,128)} %bitcast.11) | data formatting | bytes 786432

commit v4 on v3

--- a/solution.py
+++ b/solution.py
@@ -29,7 +29,7 @@
     (
         b_own, a_all, prod, quarter_acc, own_core, core_in_0, core_in_1, core_in_2, acc,
         packed_0, packed_1, packed_2, far_0, far_1, far_2, near_0, near_1, near_2,
-        meta, meta_a, meta_b, table_v, table_s,
+        meta_a, meta_b, table_v, table_s,
         loc_sem, tab_sem,
         ma_send, ma_recv, mb_send, mb_recv,
         bp_send, bp_recv, bm_send, bm_recv,
@@ -71,8 +71,8 @@
             device_id=device, device_id_type=pl.DeviceIdType.MESH,
         )
 
-    pairs = [(fy, rx) for fy in range(2) for rx in range(NX) if (fy, rx) != (0, 0)]
-    peers = [z_at(r) for r in range(1, NZ)] + [pair_at(*p) for p in pairs] + [other_y, sibling]
+    peers = [z_at(r) for r in (1, 2, NZ - 2, NZ - 1)] + [x_at(r) for r in range(1, NX)]
+    peers += [pair_at(1, 0), other_y, sibling]
     barrier = pltpu.get_barrier_semaphore()
     for peer in peers:
         pl.semaphore_signal(barrier, inc=1, device_id=peer, device_id_type=pl.DeviceIdType.MESH)
@@ -98,7 +98,6 @@
     for o in range(KPG):
         for t in range(TERMS):
             mine = jnp.where(spot == 128 + o * TERMS + t, b_cols_ref[t, 0, o], mine)
-    meta[...] = mine
     meta_b[0] = mine
     meta_a[0] = mine
 
@@ -144,6 +143,8 @@
         sems = (bp_send, bp_recv) if sign > 0 else (bm_send, bm_recv)
         split = HALF_CUT if h == 0 else QUARTER_CUT
         lo, hi = (0, split) if (n == 0) == (sign > 0) else (split, BLOCKS)
+        if h == 1 and k < 3:
+            lo, hi = 0, BLOCKS
         index = h * 8 + k * 2 + n
         hops[h, sign, k, n] = go(copy(
             bufs[h][(-sign * k) % NZ].at[pl.ds(lo, hi - lo)],
@@ -152,7 +153,7 @@
         ))
 
     def begin(h):
-        for n in range(2):
+        for n in range(1 if h == 1 else 2):
             hop(h, 1, 0, n)
             hop(h, -1, 0, n)
 
@@ -196,11 +197,19 @@
         for c in xs[:4]:
             c.start()
 
-    to_z = [go(copy(meta, meta_b.at[r], mb_send.at[r], mb_recv.at[r], z_at(r))) for r in range(1, NZ)]
-    to_pair = [
-        go(copy(meta, meta_a.at[fy * NX + rx], ma_send.at[fy * NX + rx], ma_recv.at[fy * NX + rx], pair_at(fy, rx)))
-        for fy, rx in pairs
-    ]
+    on_z, on_a = {}, {}
+
+    def index_z(src, dst, step):
+        on_z[dst] = go(copy(meta_b.at[src], meta_b.at[dst], mb_send.at[dst], mb_recv.at[dst], z_at(step)))
+
+    def index_a(src, dst, device):
+        on_a[dst] = go(copy(meta_a.at[src], meta_a.at[dst], ma_send.at[dst], ma_recv.at[dst], device))
+
+    index_a(0, NX, pair_at(1, 0))
+    for r in (1, 2, NZ - 2, NZ - 1):
+        index_z(0, r, r)
+    for r in range(1, NX):
+        index_a(0, r, x_at(r))
 
     forward(0, 1, 0)
 
@@ -214,10 +223,21 @@
     sent.extend(xs[:4])
     go(ts[0])
     forward(0, 1, 1)
+    on_z[2].wait_recv()
+    index_z(2, 4, 2)
+    on_z[1].wait_recv()
+    index_z(1, 3, 2)
+    on_z[NZ - 1].wait_recv()
+    index_z(NZ - 1, 5, NZ - 2)
+    on_a[NX].wait_recv()
+    for r in range(1, NX):
+        index_a(NX, NX + r, x_at(r))
     forward(1, 1, 0)
-    forward(1, 1, 1)
-
-    for c in to_z + to_pair:
+
+    forward(0, 2, 0)
+    forward(0, 2, 1)
+    forward(1, 2, 0)
+    for c in [on_z[r] for r in (3, 4, 5, 6)] + [on_a[r] for r in (1, 2, 3, 5, 6, 7)]:
         c.wait_recv()
     b_cols = jnp.concatenate([meta_b[(NZ - d) % NZ, 1:2, :] for d in range(NZ)], axis=0)
     away = (lane // 32 - x + NX) % NX
@@ -263,16 +283,12 @@
     to_scalar.start()
     to_scalar.wait()
 
-    forward(0, 2, 0)
-    forward(0, 2, 1)
-    forward(1, 2, 0)
-    forward(1, 2, 1)
     xs[0].wait_recv()
     go(xs[4])
     xs[1].wait_recv()
     go(xs[5])
+    begin(2)
     forward(0, 3, 0)
-    begin(2)
     forward(0, 3, 1, False)
     xs[2].wait_recv()
     go(ts[1])
@@ -415,7 +431,6 @@
     xs[5].wait_recv()
     go(ts[3])
     forward(1, 3, 0)
-    forward(1, 3, 1, False)
     for c in ts:
         c.wait_recv()
     multiply_all(0, 0, 1, 7)
@@ -497,7 +512,6 @@
             thin(4 * ROWS), slim(4 * ROWS), slim(4 * ROWS),
             thin(ROWS), slim(ROWS), slim(ROWS),
             thin(2 * ROWS), slim(2 * ROWS), slim(2 * ROWS),
-            pltpu.VMEM((8, 128), jnp.int32),
             pltpu.VMEM((8, 8, 128), jnp.int32),
             pltpu.VMEM((8, 8, 128), jnp.int32),
             pltpu.VMEM((2, 8, 128), jnp.int32),

time: 101 us -> 100 us (0.990)
  no operation moved by 1% of the time
where the time goes in v4:
time: 100 us
  Pallas kernels  98.5 us (98%)
  local copies, waits for them, and re-layouts  1.77 us (2%)
    pallas_call x1, Pallas kernels, local(): pl.pallas_call(kernel, out_shape=jax.ShapeDtypeStruct((ROWS, 128, 128), j...  98.5 us

profile of v4, /device:TPU:1, one launch (start us, length us, event | category | flops | bytes accessed | tf_op | source)
XLA Modules:
  0.0 100.3 jit_solution(18346603417805315804)
XLA Ops:
  0.0 98.5 %shard_map.64 = f32[6,128,128]{2,1,0:T(8,128)} custom-call(s32[3,1,6]{2,1,0:T(1,128)} %bitcast.16, s32[3,6]{1,0:T(4,128)} %bitcast.14, s32[3,1,5]{2,1,0:T(1,128)} %bitcast.17, s32[4,6]{1,0:T(4,128)} %bitcast.15, f32[18,128,128]{2,1,0:T(8,128)} %bitcast.12, f32[15,128,128]{2,1,0:T(8,128)} %bitcast.13), custom_call_target="tpu_custom_call" | custom-call | flops 2000000000 | bytes 3000000 | tf_op jit(solution)/shard_map/pallas_call | solution.py:500
  98.5 1.8 %copy.9 = f32[6,1,1,128,128]{4,3,2,1,0:T(8,128)} copy(f32[6,1,1,128,128]{4,3,2,1,0:T(8,128)} %bitcast.11) | data formatting | bytes 786432
